TPU v7x, 32 devices: a whole 2x2x4 slice. The times are simulated.
32 devices in a mesh: gx: 4 (over z), gy: 4 (over x, core), gz: 2 (over y).
Axes of the slice: x: 2, y: 2, z: 4, core: 2. Of those that a mesh axis runs over, the one named last changes fastest.
Arguments:
- right_side: float32 [16, 32, 256], P('gx', 'gy', 'gz'), may hold values from -8 to 8
- diagonal: float32 [16, 32, 256], P('gx', 'gy', 'gz'), may hold values from 0.2 to 2
- sign_bits: int32 [16, 32, 256], P('gx', 'gy', 'gz'), may hold values from 0 to 1
- freq_x: int32 [2048], replicated, may hold values from 0 to 15
- freq_y: int32 [2048], replicated, may hold values from 0 to 31
- freq_z: int32 [2048], replicated, may hold values from 0 to 255
Outputs:
- solution_field: float32 [16, 32, 256], P('gx', 'gy', 'gz')
- residual: float32 [16, 32, 256], P('gx', 'gy', 'gz')
All inputs are finite; a program needn't handle non-finite values.
Results may differ from a plain program's by a relative error of at most 0.0009.
Values sent between devices are 32-bit elements; how exact they have to be, the bound alone decides.
A program may use at most 64 MiB of HBM per device.

v0:
```python
import jax
import jax.numpy as jnp
from jax import lax
from jax.sharding import PartitionSpec as P

BASIS = 8
ITERS = 2


center_value = 7.0
half_range = 7.0
tiny_value = 1e-06
highest = lax.Precision.HIGHEST


def extended(shard, sides, width):
    for axis, dim in sides:
        size, length = (lax.axis_size(axis), shard.shape[dim])
        up = [(i, (i + 1) % size) for i in range(size - 1)]
        down = [(j, i) for i, j in up]
        last = lax.slice_in_dim(shard, length - width, length, axis=dim)
        first = lax.slice_in_dim(shard, 0, width, axis=dim)
        before = lax.ppermute(last, axis, up)
        after = lax.ppermute(first, axis, down)
        shard = jnp.concatenate([before, shard, after], axis=dim)
    return shard


def stencil(padded, diagonal):
    beside = padded[2:, 1:-1, 1:-1] + padded[:-2, 1:-1, 1:-1]
    beside = beside + padded[1:-1, 2:, 1:-1] + padded[1:-1, :-2, 1:-1]
    beside = beside + padded[1:-1, 1:-1, 2:] + padded[1:-1, 1:-1, :-2]
    return (6.0 + diagonal) * padded[1:-1, 1:-1, 1:-1] - beside


def cosine_table(freqs, offset, count, length):
    indices = offset + jnp.arange(count, dtype=jnp.int32)
    phases = (2 * indices[:, None] + 1) * freqs[None, :] % (4 * length)
    return (jnp.sqrt(2.0 / length) * jnp.cos(jnp.pi * phases / (2.0 * length))).astype(jnp.float32)


def least_squares(matrix):
    count = matrix.shape[0] - 1
    target = matrix[count]
    orthonormal = []
    upper = {}
    for column_at in range(count):
        column = matrix[column_at]
        for repeat in range(2):
            for earlier in range(column_at):
                amount = jnp.dot(orthonormal[earlier], column, precision=highest)
                column = column - amount * orthonormal[earlier]
                upper[earlier, column_at] = upper.get((earlier, column_at), 0.0) + amount
        length = jnp.sqrt(jnp.dot(column, column, precision=highest) + tiny_value)
        orthonormal.append(column / length)
        upper[column_at, column_at] = length
    projected = [jnp.dot(basis_row, target, precision=highest) for basis_row in orthonormal]
    solved = [None] * count
    for row_at in range(count - 1, -1, -1):
        value = projected[row_at]
        for later in range(row_at + 1, count):
            value = value - upper[row_at, later] * solved[later]
        solved[row_at] = value / upper[row_at, row_at]
    return jnp.stack(solved)


def basis_plain(residual, diagonal):
    vectors = [residual]
    images = []
    for position in range(BASIS):
        padded = extended(vectors[position], (("gx", 0), ("gy", 1), ("gz", 2)), 1)
        image = stencil(padded, diagonal)
        images.append(image)
        if position + 1 < BASIS:
            turned = (image - center_value * vectors[position]) / half_range
            vectors.append(turned if position == 0 else 2.0 * turned - vectors[position - 1])
    return (vectors, images)


def local_sketch(columns, signs, table_x, table_y, table_z):
    flipped = jnp.stack(columns, axis=2) * signs[:, :, None, :]
    size_x, size_y, count, depth = flipped.shape
    rows_flat = flipped.reshape(-1, depth)
    weights = table_x[:, None, :] * table_y[None, :, :]
    sampled = table_z.shape[1]
    block = min(512, sampled)
    pieces = []
    for begin in range(0, sampled, block):
        inner_sums = jnp.dot(
            rows_flat,
            table_z[:, begin : begin + block],
            precision=highest,
            preferred_element_type=jnp.float32,
        )
        inner_sums = inner_sums.reshape(size_x, size_y, count, block)
        pieces.append(
            jnp.einsum(
                "xyjs,xys->js", inner_sums, weights[:, :, begin : begin + block], precision=highest
            )
        )
    return jnp.concatenate(pieces, axis=1)


def shards(right_side, diagonal, sign_bits, freq_x, freq_y, freq_z):
    size_x, size_y, size_z = right_side.shape
    table_x = cosine_table(
        freq_x, lax.axis_index("gx") * size_x, size_x, size_x * lax.axis_size("gx")
    )
    table_y = cosine_table(
        freq_y, lax.axis_index("gy") * size_y, size_y, size_y * lax.axis_size("gy")
    )
    table_z = cosine_table(
        freq_z, lax.axis_index("gz") * size_z, size_z, size_z * lax.axis_size("gz")
    )
    signs = 1.0 - 2.0 * sign_bits.astype(jnp.float32)
    solution = jnp.zeros_like(right_side)
    residual = right_side
    for restart in range(ITERS):
        vectors, images = basis_plain(residual, diagonal)
        partial_value = local_sketch(images + [residual], signs, table_x, table_y, table_z)
        shares = lax.psum_scatter(partial_value, "gx", scatter_dimension=1, tiled=True)
        shares = lax.psum(shares, ("gy", "gz"))
        matrix = lax.all_gather(shares, "gx", axis=1, tiled=True)
        weights_solved = least_squares(matrix)
        for position in range(BASIS):
            solution = solution + weights_solved[position] * vectors[position]
            residual = residual - weights_solved[position] * images[position]
    return (solution, residual)


def solution(mesh):
    in_specs = (P("gx", "gy", "gz"), P("gx", "gy", "gz"), P("gx", "gy", "gz"), P(), P(), P())
    out_specs = (P("gx", "gy", "gz"), P("gx", "gy", "gz"))
    return jax.shard_map(shards, mesh=mesh, in_specs=in_specs, out_specs=out_specs, check_vma=False)
```

profile of v0, /device:TPU:0, one launch (start us, length us, event | category | flops | bytes accessed | tf_op | source)
XLA Modules:
  0.0 724.9 jit_solution(14029988108474382836)
XLA Ops:
  7.9 4.9 collective-permute-start.1
  14.2 4.2 collective-permute-done
  21.0 3.5 collective-permute-done.2
  25.8 4.5 collective-permute-start.5
  32.3 3.5 collective-permute-start.7
  37.1 4.2 collective-permute-done.6
  44.6 3.5 collective-permute-done.8
  49.5 4.5 collective-permute-start.11
  55.9 3.5 collective-permute-start.13
  60.7 4.2 collective-permute-done.12
  64.9 2.0 collective-permute-start.15
  68.2 3.5 collective-permute-done.14
  73.2 4.5 collective-permute-start.17
  82.8 4.2 collective-permute-done.18
  90.3 3.5 collective-permute-done.20
  95.3 4.5 collective-permute-start.23
  104.9 4.2 collective-permute-done.24
  109.1 2.0 collective-permute-start.27
  112.4 3.5 collective-permute-done.26
  117.4 4.5 collective-permute-start.29
  127.0 4.2 collective-permute-done.30
  131.2 2.0 collective-permute-start.33
  134.5 3.9 fusion.19
  139.8 4.5 collective-permute-start.35
  149.8 3.8 collective-permute-done.36
  153.7 2.2 collective-permute-start.39
  157.3 5.5 collective-permute-done.38
  164.2 4.5 collective-permute-start.41
  173.9 4.2 collective-permute-done.42
  181.4 3.5 collective-permute-done.44
  186.3 4.7 collective-permute-start.47
  197.5 19.1 %reduce-scatter.3.cloned.1.call-done = f32[9,512]{1,0:T(8,128)} async-done(((f32[9,2048]{1,0:T(8,128)}), f32[9,512]{1,0:T(8,128)}) %reduce-scatter.3.cloned.1.call-update) | async-done | bytes 18448 | tf_op jit(solution)/shard_map/reduce_scatter | solution.py:121
  216.6 24.6 %psum.14 = f32[9,512]{1,0:T(8,128)S(1)} all-reduce(f32[9,512]{1,0:T(8,128)} %reduce-scatter.3.cloned.1.call-done), channel_id=1, replica_groups=mesh['gx'=4,'gy'=4,'gz'=2] {'gy','gz'}, use_global_device_ids=true, to_apply=%region_1.2 | all-reduce | flops 4608 | bytes 36864 | tf_op jit(solution)/shard_map/psum | solution.py:122
  241.2 13.4 %all_gather.6 = f32[9,2048]{1,0:T(8,128)S(1)} all-gather(f32[9,512]{1,0:T(8,128)S(1)} %psum.14), channel_id=1, replica_groups=mesh['gx'=4,'gy'=4,'gz'=2] {'gx'}, dimensions={1}, use_global_device_ids=true | all-gather | bytes 92160 | tf_op jit(solution)/shard_map/all_gather | solution.py:123
  369.0 4.2 collective-permute-done.48
  375.7 3.4 collective-permute-done.50
  380.5 4.5 collective-permute-start.53
  386.9 3.7 collective-permute-start.55
  391.9 4.2 collective-permute-done.54
  399.5 3.5 collective-permute-done.56
  404.4 4.5 collective-permute-start.59
  410.8 2.5 collective-permute-start.61
  414.6 4.2 collective-permute-done.60
  422.1 3.5 collective-permute-done.62
  427.1 4.5 collective-permute-start.65
  436.7 4.2 collective-permute-done.66
  440.9 2.0 collective-permute-start.69
  444.2 3.5 collective-permute-done.68
  449.2 4.5 collective-permute-start.71
  458.8 4.2 collective-permute-done.72
  466.3 3.5 collective-permute-done.74
  471.3 4.5 collective-permute-start.77
  480.9 4.2 collective-permute-done.78
  488.4 3.5 collective-permute-done.80
  493.3 4.5 collective-permute-start.83
  503.0 4.2 collective-permute-done.84
  510.5 3.5 collective-permute-done.86
  515.4 4.5 collective-permute-start.89
  525.1 4.2 collective-permute-done.90
  532.6 3.5 collective-permute-done.92
  537.5 4.8 collective-permute-start.95
  548.6 19.2 %reduce-scatter.5.cloned.1.call-done = f32[9,512]{1,0:T(8,128)} async-done(((f32[9,2048]{1,0:T(8,128)}), f32[9,512]{1,0:T(8,128)}) %reduce-scatter.5.cloned.1.call-update) | async-done | bytes 18448 | tf_op jit(solution)/shard_map/reduce_scatter | solution.py:121
  567.8 24.6 %psum.15 = f32[9,512]{1,0:T(8,128)S(1)} all-reduce(f32[9,512]{1,0:T(8,128)} %reduce-scatter.5.cloned.1.call-done), channel_id=1, replica_groups=mesh['gx'=4,'gy'=4,'gz'=2] {'gy','gz'}, use_global_device_ids=true, to_apply=%region_3.4 | all-reduce | flops 4608 | bytes 36864 | tf_op jit(solution)/shard_map/psum | solution.py:122
  592.4 13.4 %all_gather.7 = f32[9,2048]{1,0:T(8,128)S(1)} all-gather(f32[9,512]{1,0:T(8,128)S(1)} %psum.15), channel_id=1, replica_groups=mesh['gx'=4,'gy'=4,'gz'=2] {'gx'}, dimensions={1}, use_global_device_ids=true | all-gather | bytes 92160 | tf_op jit(solution)/shard_map/all_gather | solution.py:123
  (449 shorter events, 273.7 us)
Async XLA Ops:
  7.2 209.4 %reduce-scatter.3.cloned.1.call-start = ((), (), s32[]{:S(2)}) async-start(), calls=%async_computation.2 | async-start | bytes 163840 | tf_op jit(solution)/shard_map/reduce_scatter | solution.py:121
  7.9 6.2 collective-permute-start.1
  12.9 5.5 collective-permute-start
  24.6 6.0 collective-permute-start.4
  25.8 6.3 collective-permute-start.5
  35.7 5.5 collective-permute-start.6
  43.3 4.9 collective-permute-start.8
  48.2 6.0 collective-permute-start.10
  49.5 6.3 collective-permute-start.11
  59.4 5.5 collective-permute-start.12
  66.9 4.9 collective-permute-start.14
  71.9 6.0 collective-permute-start.16
  73.2 6.3 collective-permute-start.17
  81.5 5.5 collective-permute-start.18
  89.0 4.9 collective-permute-start.20
  94.0 6.0 collective-permute-start.22
  95.3 6.3 collective-permute-start.23
  103.6 5.5 collective-permute-start.24
  111.1 4.9 collective-permute-start.26
  116.1 6.0 collective-permute-start.28
  117.4 6.3 collective-permute-start.29
  125.7 5.5 collective-permute-start.30
  131.2 7.2 collective-permute-start.33
  133.2 5.2 collective-permute-start.32
  138.5 6.0 collective-permute-start.34
  139.8 6.3 collective-permute-start.35
  148.2 5.5 collective-permute-start.36
  155.9 6.9 collective-permute-start.38
  162.9 6.2 collective-permute-start.40
  164.2 6.3 collective-permute-start.41
  172.5 5.5 collective-permute-start.42
  180.0 4.9 collective-permute-start.44
  185.0 6.1 collective-permute-start.46
  186.3 6.3 collective-permute-start.47
  197.4 370.4 %reduce-scatter.5.cloned.1.call-start = ((), (), s32[]{:S(2)}) async-start(), calls=%async_computation.3 | async-start | bytes 163840 | tf_op jit(solution)/shard_map/reduce_scatter | solution.py:121
  367.6 5.5 collective-permute-start.48
  379.2 6.0 collective-permute-start.52
  380.5 6.3 collective-permute-start.53
  386.9 5.0 collective-permute-start.55
  390.6 5.5 collective-permute-start.54
  398.2 4.9 collective-permute-start.56
  403.1 6.0 collective-permute-start.58
  404.4 6.3 collective-permute-start.59
  413.3 5.5 collective-permute-start.60
  420.8 4.9 collective-permute-start.62
  425.8 6.0 collective-permute-start.64
  427.1 6.3 collective-permute-start.65
  435.4 5.5 collective-permute-start.66
  442.9 4.9 collective-permute-start.68
  447.9 6.0 collective-permute-start.70
  449.2 6.3 collective-permute-start.71
  457.5 5.5 collective-permute-start.72
  470.0 6.0 collective-permute-start.76
  471.3 6.3 collective-permute-start.77
  479.6 5.5 collective-permute-start.78
  492.1 6.0 collective-permute-start.82
  493.3 6.3 collective-permute-start.83
  501.7 5.5 collective-permute-start.84
  514.1 6.0 collective-permute-start.88
  515.4 6.3 collective-permute-start.89
  523.8 5.5 collective-permute-start.90
  531.3 4.9 collective-permute-start.92
  536.2 6.1 collective-permute-start.94
  537.5 6.3 collective-permute-start.95
  (40 other events, 154.5 us)
Sparse Core Ops, SparseCore 0:
  197.5 18.9 reduce-scatter.2
  548.8 18.9 reduce-scatter.4
where the time goes:
time: 730 us; the launch traced here: 725 us
  starting transfers between devices  204 us (28%)
  waiting for transfers between devices  187 us (26%)
  other arithmetic  138 us (19%)
  between operations  110 us (15%)
  blocking collectives  76 us (10%)
  matrix products  8.01 us (1%)
    ppermute x48, starting transfers between devices, extended(): before = lax.ppermute(last, axis, up)  142 us
    ppermute x48, waiting for transfers between devices, extended(): after = lax.ppermute(first, axis, down)  123 us
    sub x70, other arithmetic, least_squares(): column = column - amount * orthonormal[earlier]  72.4 us
    ppermute x48, starting transfers between devices, extended(): after = lax.ppermute(first, axis, down)  61.9 us
    psum x2, blocking collectives, shards(): shares = lax.psum(shares, ('gy', 'gz'))  49.2 us
    dot_general x70, other arithmetic, least_squares(): amount = jnp.dot(orthonormal[earlier], column, precision=highest)  44.8 us
    reduce_scatter x2, waiting for transfers between devices, shards(): lax.psum_scatter(partial_value, 'gx', scatter_dimension=1, tiled=True)  38.3 us
    all_gather x2, blocking collectives, shards(): matrix = lax.all_gather(shares, 'gx', axis=1, tiled=True)  26.7 us
  transfers between devices with their start and end apart: 98, of which 62 were waited for; matrix products, arithmetic and copies ran while one was open for 1% of the time, Pallas kernels for 0%

commit v1 on v0

--- a/solution.py
+++ b/solution.py
@@ -1,6 +1,11 @@
+import functools
+import math
+
 import jax
 import jax.numpy as jnp
 from jax import lax
+from jax.experimental import pallas as pl
+from jax.experimental.pallas import tpu as pltpu
 from jax.sharding import PartitionSpec as P
 
 BASIS = 8
@@ -128,7 +133,381 @@
     return (solution, residual)
 
 
+MESH = pl.DeviceIdType.MESH
+LANES = 128
+SINE = [(-1.0) ** k / math.factorial(2 * k + 1) for k in range(7)]
+
+
+def cosines(freqs, count, length):
+    cells = lax.broadcasted_iota(jnp.int32, (count, freqs.shape[1]), 0)
+    phases = lax.rem((2 * cells + 1) * freqs, 4 * length)
+    folded = length - jnp.minimum(phases, 4 * length - phases)
+    angle = folded.astype(jnp.float32) * (math.pi / (2.0 * length))
+    square = angle * angle
+    value = jnp.full_like(angle, SINE[-1])
+    for term in SINE[-2::-1]:
+        value = value * square + term
+    return value * angle * math.sqrt(2.0 / length)
+
+
+def total_of(value):
+    return jnp.sum(jnp.sum(value, axis=0, keepdims=True), axis=1, keepdims=True)
+
+
+def solve_rows(rows, target):
+    count = len(rows)
+    basis, among, short, upper, inverse = [], [], [], {}, []
+    for at_column in range(count):
+        column = rows[at_column]
+        for repeat in range(2):
+            left = [total_of(q * column) for q in basis]
+            amounts = []
+            for e in range(at_column):
+                amount = left[e]
+                amounts.append(amount)
+                left[e] = amount * short[e]
+                for f in range(at_column):
+                    if f != e:
+                        left[f] = left[f] - amount * among[max(e, f)][min(e, f)]
+            for e in range(at_column):
+                column = column - amounts[e] * basis[e]
+                upper[e, at_column] = upper.get((e, at_column), 0.0) + amounts[e]
+        length = jnp.sqrt(total_of(column * column) + tiny_value)
+        scale = 1.0 / length
+        basis.append(column * scale)
+        among.append([value * scale for value in left] if at_column else [])
+        short.append(tiny_value * scale * scale)
+        inverse.append(scale)
+    projected = [total_of(q * target) for q in basis]
+    solved = [None] * count
+    for row in range(count - 1, -1, -1):
+        value = projected[row]
+        for later in range(row + 1, count):
+            value = value - upper[row, later] * solved[later]
+        solved[row] = value * inverse[row]
+    return solved
+
+
+class Gather:
+    def __init__(self, sizes, block, send_sem, recv_sem):
+        self.sizes, self.block = sizes, block
+        self.send_sem, self.recv_sem = send_sem, recv_sem
+        self.count = 0
+        self.at = {axis: lax.axis_index(axis) for axis in sizes}
+        self.started = []
+
+    def regions(self, ref, state, at):
+        bx, by, bz = self.block
+        gx, gy, gz = at["gx"], at["gy"], at["gz"]
+        xs = slice(None) if state["x"] == "all" else pl.ds(gx * bx, bx)
+        zs = slice(None) if state["z"] == "all" else pl.ds(pl.multiple_of(gz * bz, bz), bz)
+        if state["y"] == "own":
+            ys = [gy]
+        else:
+            ys = [lax.rem(gy, 2) + 2 * k for k in range(self.sizes["gy"] // 2)]
+        return [ref.at[xs, pl.ds(pl.multiple_of(y * by, by), by), zs] for y in ys]
+
+    def start(self, ref, state, phase):
+        axis = {"X": "gx", "Z": "gz", "H": "gy", "C": "gy"}[phase]
+        size, here = self.sizes[axis], self.at[axis]
+        if phase == "C":
+            hops = [(here + 1 - 2 * lax.rem(here, 2), here + 1 - 2 * lax.rem(here, 2))]
+        else:
+            stride = 2 if phase == "H" else 1
+            hops = [
+                (lax.rem(here + k, size), lax.rem(here + size - k, size))
+                for k in range(stride, size, stride)
+            ]
+        arriving = []
+        for target, origin in hops:
+            mine = self.regions(ref, state, self.at)
+            theirs = self.regions(ref, state, {**self.at, axis: origin})
+            for source, landing in zip(mine, theirs):
+                n = self.count
+                self.count += 1
+                sems = dict(send_sem=self.send_sem.at[n], recv_sem=self.recv_sem.at[n])
+                go = dict(device_id={axis: target}, device_id_type=MESH)
+                copy = pltpu.make_async_remote_copy(src_ref=source, dst_ref=source, **sems, **go)
+                copy.start()
+                self.started.append(copy)
+                arriving.append(
+                    pltpu.make_async_remote_copy(src_ref=landing, dst_ref=landing, **sems, **go)
+                )
+        if phase == "X":
+            state["x"] = "all"
+        elif phase == "Z":
+            state["z"] = "all"
+        elif phase == "H":
+            state["y"] = "half"
+        else:
+            state["y"] = "all"
+        return arriving
+
+
+def copies_needed(sizes):
+    half = sizes["gy"] // 2
+    return 3 * (sizes["gx"] - 1 + (sizes["gz"] - 1) * half + half - 1 + half) + 8
+
+
+def whole_kernel(
+    sizes, share, right_ref, diagonal_ref, bits_ref, fx_ref, fy_ref, fz_ref, sol_ref, res_ref,
+    field, diag, sign, vectors, images, flipped, table, weights, rows, sums, send_sem, recv_sem,
+    small_send, small_recv,
+):
+    bx, by, bz = right_ref.shape
+    nx, ny, nz = field.shape
+    wide = table.shape[1]
+    at = {axis: lax.axis_index(axis) for axis in sizes}
+
+    barrier = pltpu.get_barrier_semaphore()
+    peers = 0
+    for axis, size in sizes.items():
+        for k in range(1, size):
+            target = lax.rem(at[axis] + k, size)
+            pl.semaphore_signal(barrier, inc=1, device_id={axis: target}, device_id_type=MESH)
+            peers += 1
+    x0 = at["gx"] * bx
+    y0 = pl.multiple_of(at["gy"] * by, by)
+    z0 = pl.multiple_of(at["gz"] * bz, bz)
+    own = (pl.ds(x0, bx), pl.ds(y0, by), pl.ds(z0, bz))
+    field[own] = right_ref[...]
+    diag[own] = diagonal_ref[...]
+    sign[own] = 1.0 - 2.0 * bits_ref[...].astype(jnp.float32)
+    pl.semaphore_wait(barrier, peers)
+
+    gather = Gather(sizes, (bx, by, bz), send_sem, recv_sem)
+    orders = [(field, "XZHC"), (diag, "XHZC"), (sign, "XZHC")]
+    states = [{"x": "own", "y": "own", "z": "own"} for _ in orders]
+
+    def begin(step):
+        arriving = []
+        for (ref, order), state in zip(orders, states):
+            arriving += gather.start(ref, state, order[step])
+        return arriving
+
+    arriving = begin(0)
+    me = (at["gx"] * sizes["gy"] + at["gy"]) * sizes["gz"] + at["gz"]
+    lane = lax.broadcasted_iota(jnp.int32, (1, LANES), 1)
+
+    def own_rows(ref):
+        begin_at = me * share
+        row = ref[pl.ds(begin_at // LANES, 1), :]
+        part = lax.rem(begin_at, LANES) // share
+        spread = row
+        for k in range(LANES // share):
+            turned = row
+            for group in range(LANES // share):
+                shift = ((group - k) * share) % LANES
+                moved = pltpu.roll(row, shift, 1) if shift else row
+                turned = jnp.where(lane // share == group, moved, turned)
+            spread = jnp.where(part == k, turned, spread)
+        return jnp.concatenate([spread] * (wide // LANES), axis=1)
+
+    group = lax.broadcasted_iota(jnp.int32, (nz, wide), 1) // share
+    cos_z = cosines(own_rows(fz_ref), nz, nz)
+    first = cos_z.astype(jnp.bfloat16).astype(jnp.float32)
+    second = (cos_z - first).astype(jnp.bfloat16).astype(jnp.float32)
+    third = cos_z - first - second
+    chosen = jnp.where(group == 0, first, jnp.where(group == 1, second, third))
+    table[...] = jnp.where(group < 3, chosen, 0.0).astype(jnp.bfloat16)
+    cos_x = cosines(own_rows(fx_ref), nx, nx)
+    cos_y = cosines(own_rows(fy_ref), ny, ny)
+    for x in range(nx):
+        weights[x] = cos_x[x : x + 1] * cos_y
+    edge = jnp.zeros((ny, nz), jnp.float32)
+    for j in range(BASIS):
+        vectors[j, 0] = edge
+        vectors[j, nx + 1] = edge
+
+    for copy in arriving:
+        copy.wait_recv()
+    for step in range(1, 4):
+        for copy in begin(step):
+            copy.wait_recv()
+
+    row_at = lax.broadcasted_iota(jnp.int32, (ny, nz), 0)
+    lane_at = lax.broadcasted_iota(jnp.int32, (ny, nz), 1)
+
+    def put_flipped(x, plane):
+        turned = plane * sign[x]
+        high = turned.astype(jnp.bfloat16)
+        flipped[0, x] = high
+        flipped[1, x] = (turned - high.astype(jnp.float32)).astype(jnp.bfloat16)
+
+    def sketch_row(j):
+        cells = nx * ny
+        both = flipped[...].reshape(2 * cells, nz)
+        sampled = jnp.dot(both, table[...], preferred_element_type=jnp.float32)
+        sampled = (sampled[:cells] + sampled[cells:]) * weights[...].reshape(cells, wide)
+        total = jnp.sum(sampled, axis=0, keepdims=True)
+        folded = total[:, :LANES]
+        for k in range(1, wide // LANES):
+            folded = folded + total[:, k * LANES : (k + 1) * LANES]
+        spread = folded
+        for k in range(1, LANES // share):
+            spread = spread + pltpu.roll(folded, k * share, 1)
+        rows[pl.ds(j, 1), :] = spread
+
+    small = 0
+    for restart in range(ITERS):
+
+        @pl.loop(0, nx)
+        def _(x):
+            plane = field[x]
+            vectors[0, x + 1] = plane
+            put_flipped(x, plane)
+
+        sketch_row(BASIS)
+
+        @pl.loop(0, BASIS)
+        def _(j):
+            before = jnp.maximum(j - 1, 0)
+            after = jnp.minimum(j + 1, BASIS - 1)
+            step = jnp.where(j == 0, 1.0 / half_range, 2.0 / half_range).astype(jnp.float32)
+            old = jnp.where(j == 0, 0.0, 1.0).astype(jnp.float32)
+
+            @pl.loop(0, nx, unroll=2)
+            def _(x):
+                here = vectors[j, x + 1]
+                beside = vectors[j, x + 2] + vectors[j, x]
+                beside = beside + jnp.where(row_at < ny - 1, pltpu.roll(here, ny - 1, 0), 0.0)
+                beside = beside + jnp.where(row_at > 0, pltpu.roll(here, 1, 0), 0.0)
+                beside = beside + jnp.where(lane_at < nz - 1, pltpu.roll(here, nz - 1, 1), 0.0)
+                beside = beside + jnp.where(lane_at > 0, pltpu.roll(here, 1, 1), 0.0)
+                image = (6.0 + diag[x]) * here - beside
+                images[j, x] = image
+                put_flipped(x, image)
+                turned = (image - center_value * here) * step - old * vectors[before, x + 1]
+
+                @pl.when(j < BASIS - 1)
+                def _():
+                    vectors[after, x + 1] = turned
+
+            sketch_row(j)
+
+        buffer = sums.at[restart]
+        behind = (lane // share == 1) & (lax.broadcasted_iota(jnp.int32, (BASIS, LANES), 0) == 0)
+        tile = jnp.where(behind, rows[BASIS : BASIS + 1, :], rows[0:BASIS, :])
+        buffer[pl.ds(at["gy"], 1), pl.ds(at["gx"], 1), pl.ds(at["gz"], 1)] = tile.reshape(
+            1, 1, 1, BASIS, LANES
+        )
+        whole = {axis: False for axis in sizes}
+        for axis in ("gy", "gx", "gz"):
+            here, size = at[axis], sizes[axis]
+            arrivals = []
+            for k in range(1, size):
+                target, origin = lax.rem(here + k, size), lax.rem(here + size - k, size)
+                sems = dict(send_sem=small_send.at[small], recv_sem=small_recv.at[small])
+                go = dict(device_id={axis: target}, device_id_type=MESH)
+                small += 1
+                source, landing = (
+                    buffer.at[
+                        tuple(
+                            slice(None) if whole[name] else pl.ds(place[name], 1)
+                            for name in ("gy", "gx", "gz")
+                        )
+                    ]
+                    for place in (at, {**at, axis: origin})
+                )
+                copy = pltpu.make_async_remote_copy(src_ref=source, dst_ref=source, **sems, **go)
+                copy.start()
+                gather.started.append(copy)
+                arrivals.append(
+                    pltpu.make_async_remote_copy(src_ref=landing, dst_ref=landing, **sems, **go)
+                )
+            for copy in arrivals:
+                copy.wait_recv()
+            whole[axis] = True
+        devices = math.prod(sizes.values())
+        tiles = buffer[...].reshape(devices, BASIS, LANES)
+        sketched = [jnp.where(lane < share, tiles[:, j, :], 0.0) for j in range(BASIS)]
+        aside = pltpu.roll(tiles[:, 0, :], LANES - share, 1)
+        solved = solve_rows(sketched, jnp.where(lane < share, aside, 0.0))
+
+        kept = (pl.ds(x0 + 1, bx), pl.ds(y0, by), pl.ds(z0, bz))
+        total = jnp.zeros((bx, by, bz), jnp.float32) if restart == 0 else sol_ref[...]
+        for j in range(BASIS):
+            total = total + solved[j].reshape(1, 1, 1) * vectors[(j,) + kept]
+        sol_ref[...] = total
+        if restart == ITERS - 1:
+            left = field[own]
+            for j in range(BASIS):
+                left = left - solved[j].reshape(1, 1, 1) * images[(j,) + own]
+            res_ref[...] = left
+        else:
+            for copy in gather.started:
+                copy.wait_send()
+            gather.started = []
+
+            @pl.loop(0, nx)
+            def _(x):
+                left = field[x]
+                for j in range(BASIS):
+                    left = left - solved[j] * images[j, x]
+                field[x] = left
+
+    for copy in gather.started:
+        copy.wait_send()
+
+
+def whole_fits(sizes, nx, ny, nz, sampled):
+    devices = math.prod(sizes.values())
+    share = sampled // devices
+    if sizes["gy"] % 2 or sampled % devices or share == 0 or LANES % share or 2 * share > LANES:
+        return False
+    if nz % LANES or nz // sizes["gz"] != LANES or (ny // sizes["gy"]) % 8 or ny % 16:
+        return False
+    return nx * ny * nz * 4 * (2 * BASIS + 8) <= 24 * 1024 * 1024
+
+
+def whole_shards(sizes, right_side, diagonal, sign_bits, freq_x, freq_y, freq_z):
+    block = right_side.shape
+    nx, ny, nz = (size * sizes[axis] for size, axis in zip(block, ("gx", "gy", "gz")))
+    share = freq_x.shape[0] // math.prod(sizes.values())
+    wide = -(-3 * share // LANES) * LANES
+    freqs = [f.reshape(-1, LANES) for f in (freq_x, freq_y, freq_z)]
+    f32 = jnp.float32
+    copies = copies_needed(sizes)
+    smalls = ITERS * sum(size - 1 for size in sizes.values())
+    return pl.pallas_call(
+        functools.partial(whole_kernel, sizes, share),
+        out_shape=[jax.ShapeDtypeStruct(block, f32)] * 2,
+        in_specs=[pl.BlockSpec(memory_space=pltpu.VMEM)] * 6,
+        out_specs=[pl.BlockSpec(memory_space=pltpu.VMEM)] * 2,
+        scratch_shapes=[
+            pltpu.VMEM((nx, ny, nz), f32),
+            pltpu.VMEM((nx, ny, nz), f32),
+            pltpu.VMEM((nx, ny, nz), f32),
+            pltpu.VMEM((BASIS, nx + 2, ny, nz), f32),
+            pltpu.VMEM((BASIS, nx, ny, nz), f32),
+            pltpu.VMEM((2, nx, ny, nz), jnp.bfloat16),
+            pltpu.VMEM((nz, wide), jnp.bfloat16),
+            pltpu.VMEM((nx, ny, wide), f32),
+            pltpu.VMEM((16, LANES), f32),
+            pltpu.VMEM((ITERS, sizes["gy"], sizes["gx"], sizes["gz"], BASIS, LANES), f32),
+            pltpu.SemaphoreType.DMA((copies,)),
+            pltpu.SemaphoreType.DMA((copies,)),
+            pltpu.SemaphoreType.DMA((smalls,)),
+            pltpu.SemaphoreType.DMA((smalls,)),
+        ],
+        compiler_params=pltpu.CompilerParams(
+            collective_id=0, has_side_effects=True, vmem_limit_bytes=40 * 1024 * 1024
+        ),
+    )(right_side, diagonal, sign_bits, *freqs)
+
+
 def solution(mesh):
     in_specs = (P("gx", "gy", "gz"), P("gx", "gy", "gz"), P("gx", "gy", "gz"), P(), P(), P())
     out_specs = (P("gx", "gy", "gz"), P("gx", "gy", "gz"))
-    return jax.shard_map(shards, mesh=mesh, in_specs=in_specs, out_specs=out_specs, check_vma=False)
+    sizes = {axis: mesh.shape[axis] for axis in ("gx", "gy", "gz")}
+
+    def run(right_side, diagonal, sign_bits, freq_x, freq_y, freq_z):
+        plan = shards
+        if whole_fits(sizes, *right_side.shape, freq_x.shape[0]):
+            plan = functools.partial(whole_shards, sizes)
+        mapped = jax.shard_map(
+            plan, mesh=mesh, in_specs=in_specs, out_specs=out_specs, check_vma=False
+        )
+        return mapped(right_side, diagonal, sign_bits, freq_x, freq_y, freq_z)
+
+    return run

time: 730 us -> 87 us (0.12)
  starting transfers between devices: 204 us -> 0 us
  waiting for transfers between devices: 187 us -> 0 us
  other arithmetic: 138 us -> 0 us
  between operations: 110 us -> 0.65 us
  Pallas kernels: 0 us -> 80.3 us
  blocking collectives: 76 us -> 0 us
  matrix products: 8.01 us -> 0 us
    ppermute x96 -> x0, starting transfers between devices: 204 us -> none  [the longest x48 142 us: extended(): before = lax.ppermute(last, axis, up)]
    ppermute x96 -> x0, waiting for transfers between devices: 149 us -> none  [the longest x48 123 us: extended(): after = lax.ppermute(first, axis, down)]
    pallas_call x0 -> x1, Pallas kernels: none -> 80.3 us  [whole_shards(): pl.pallas_call(functools.partial(whole_kernel, sizes, share), out_shape=[...]
    sub x85 -> x0, other arithmetic: 73.2 us -> none  [the longest x70 72.4 us: least_squares(): column = column - amount * orthonormal[earlier]]
    dot_general x88 -> x0, other arithmetic: 55.8 us -> none  [the longest x70 44.8 us: least_squares(): amount = jnp.dot(orthonormal[earlier], column, precision=highest)]
    psum x2 -> x0, blocking collectives: 49.2 us -> none  [shards(): shares = lax.psum(shares, ('gy', 'gz'))]
    reduce_scatter x2 -> x0, waiting for transfers between devices: 38.3 us -> none  [shards(): lax.psum_scatter(partial_value, 'gx', scatter_dimension=1, tiled=True)]
    all_gather x2 -> x0, blocking collectives: 26.7 us -> none  [shards(): matrix = lax.all_gather(shares, 'gx', axis=1, tiled=True)]
  transfers between devices with their start and end apart: 98 -> 0, of which waited for: 62 -> 0; matrix products, arithmetic and copies ran while one was open for 1% -> 0% of each run, Pallas kernels for 0% -> 0%
where the time goes in v1:
time: 87 us; the launch traced here: 86.4 us
  Pallas kernels  80.3 us (92%)
  local copies, waits for them, and re-layouts  5.45 us (6%)
    pallas_call x1, Pallas kernels, whole_shards(): pl.pallas_call(functools.partial(whole_kernel, sizes, share), out_shape=[...  80.3 us
    unnamed x14, local copies, waits for them, and re-layouts  5.45 us

profile of v1, /device:TPU:0, one launch (start us, length us, event | category | flops | bytes accessed | tf_op | source)
XLA Modules:
  0.0 86.4 jit_solution(4755788506265225046)
XLA Ops:
  0.6 0.0 copy-start
  0.6 0.7 copy-done
  1.4 0.0 copy-start.1
  1.4 0.7 copy-done.1
  2.1 0.0 copy-start.2
  2.1 0.7 copy-done.2
  2.8 0.0 copy-start.3
  2.8 0.7 copy-done.3
  3.5 0.0 copy-start.4
  3.5 0.7 copy-done.4
  4.2 0.0 copy-start.5
  4.2 0.7 copy-done.5
  4.9 80.3 %shard_map.77 = (f32[4,8,128]{2,1,0:T(8,128)S(1)}, f32[4,8,128]{2,1,0:T(8,128)S(1)}) custom-call(f32[4,8,128]{2,1,0:T(8,128)S(1)} %copy-done, f32[4,8,128]{2,1,0:T(8,128)S(1)} %copy-done.1, s32[4,8,128]{2,1,0:T(8,128)S(1)} %copy-done.2, s32[16,128]{1,0:T(8,128)S(1)} %bitcast.3, s32[16,128]{1,0:T(8,128)S(1)} %bitcast.4, s32[16,128]{1,0:T(8,128)S(1)} %bitcast.5), custom_call_target="tpu_custom_call" | custom-call | tf_op jit(solution)/shard_map/pallas_call | solution.py:472
  85.2 0.6 copy.10
  85.8 0.6 copy.11
Async XLA Ops:
  0.6 0.7 copy-start
  1.4 0.7 copy-start.1
  2.1 0.7 copy-start.2
  2.8 0.7 copy-start.3
  3.5 0.7 copy-start.4
  4.2 0.7 copy-start.5

commit v2 on v1

--- a/solution.py
+++ b/solution.py
@@ -194,7 +194,6 @@
         self.send_sem, self.recv_sem = send_sem, recv_sem
         self.count = 0
         self.at = {axis: lax.axis_index(axis) for axis in sizes}
-        self.started = []
 
     def regions(self, ref, state, at):
         bx, by, bz = self.block
@@ -207,7 +206,7 @@
             ys = [lax.rem(gy, 2) + 2 * k for k in range(self.sizes["gy"] // 2)]
         return [ref.at[xs, pl.ds(pl.multiple_of(y * by, by), by), zs] for y in ys]
 
-    def start(self, ref, state, phase):
+    def plan(self, ref, state, phase):
         axis = {"X": "gx", "Z": "gz", "H": "gy", "C": "gy"}[phase]
         size, here = self.sizes[axis], self.at[axis]
         if phase == "C":
@@ -218,7 +217,7 @@
                 (lax.rem(here + k, size), lax.rem(here + size - k, size))
                 for k in range(stride, size, stride)
             ]
-        arriving = []
+        sends, arriving = [], []
         for target, origin in hops:
             mine = self.regions(ref, state, self.at)
             theirs = self.regions(ref, state, {**self.at, axis: origin})
@@ -227,9 +226,9 @@
                 self.count += 1
                 sems = dict(send_sem=self.send_sem.at[n], recv_sem=self.recv_sem.at[n])
                 go = dict(device_id={axis: target}, device_id_type=MESH)
-                copy = pltpu.make_async_remote_copy(src_ref=source, dst_ref=source, **sems, **go)
-                copy.start()
-                self.started.append(copy)
+                sends.append(
+                    pltpu.make_async_remote_copy(src_ref=source, dst_ref=source, **sems, **go)
+                )
                 arriving.append(
                     pltpu.make_async_remote_copy(src_ref=landing, dst_ref=landing, **sems, **go)
                 )
@@ -241,7 +240,7 @@
             state["y"] = "half"
         else:
             state["y"] = "all"
-        return arriving
+        return sends, arriving
 
 
 def copies_needed(sizes):
@@ -251,14 +250,35 @@
 
 def whole_kernel(
     sizes, share, right_ref, diagonal_ref, bits_ref, fx_ref, fy_ref, fz_ref, sol_ref, res_ref,
-    field, diag, sign, vectors, images, flipped, table, weights, rows, sums, send_sem, recv_sem,
-    small_send, small_recv,
+    images, diag, sign, vectors, table, weights, rows, sums, bits, freqs, load_sem, send_sem,
+    recv_sem, small_send, small_recv,
 ):
     bx, by, bz = right_ref.shape
-    nx, ny, nz = field.shape
+    _, nx, ny, nz = images.shape
     wide = table.shape[1]
+    cells = nx * ny
     at = {axis: lax.axis_index(axis) for axis in sizes}
-
+    x0 = at["gx"] * bx
+    y0 = pl.multiple_of(at["gy"] * by, by)
+    z0 = pl.multiple_of(at["gz"] * bz, bz)
+    own = (pl.ds(x0, bx), pl.ds(y0, by), pl.ds(z0, bz))
+    field = images.at[BASIS]
+
+    loads = [
+        pltpu.make_async_copy(source, target, load_sem.at[n])
+        for n, (source, target) in enumerate(
+            [
+                (right_ref, field.at[own]),
+                (diagonal_ref, diag.at[own]),
+                (bits_ref, bits),
+                (fx_ref, freqs.at[0]),
+                (fy_ref, freqs.at[1]),
+                (fz_ref, freqs.at[2]),
+            ]
+        )
+    ]
+    for copy in loads:
+        copy.start()
     barrier = pltpu.get_barrier_semaphore()
     peers = 0
     for axis, size in sizes.items():
@@ -266,32 +286,38 @@
             target = lax.rem(at[axis] + k, size)
             pl.semaphore_signal(barrier, inc=1, device_id={axis: target}, device_id_type=MESH)
             peers += 1
-    x0 = at["gx"] * bx
-    y0 = pl.multiple_of(at["gy"] * by, by)
-    z0 = pl.multiple_of(at["gz"] * bz, bz)
-    own = (pl.ds(x0, bx), pl.ds(y0, by), pl.ds(z0, bz))
-    field[own] = right_ref[...]
-    diag[own] = diagonal_ref[...]
-    sign[own] = 1.0 - 2.0 * bits_ref[...].astype(jnp.float32)
+
+    gather = Gather(sizes, (bx, by, bz), send_sem, recv_sem)
+    plans = []
+    for ref, order in [(field, "XZHC"), (diag, "XHZC"), (sign, "XZHC")]:
+        state = {"x": "own", "y": "own", "z": "own"}
+        plans.append([gather.plan(ref, state, phase) for phase in order])
+
+    def begin(array, step):
+        for copy in plans[array][step][0]:
+            copy.start()
+
+    def arrive(array, step):
+        for copy in plans[array][step][1]:
+            copy.wait_recv()
+
+    for copy in loads[:2]:
+        copy.wait()
     pl.semaphore_wait(barrier, peers)
-
-    gather = Gather(sizes, (bx, by, bz), send_sem, recv_sem)
-    orders = [(field, "XZHC"), (diag, "XHZC"), (sign, "XZHC")]
-    states = [{"x": "own", "y": "own", "z": "own"} for _ in orders]
-
-    def begin(step):
-        arriving = []
-        for (ref, order), state in zip(orders, states):
-            arriving += gather.start(ref, state, order[step])
-        return arriving
-
-    arriving = begin(0)
+    begin(0, 0)
+    begin(1, 0)
+    for copy in loads[2:]:
+        copy.wait()
+    sol_ref[...] = jnp.zeros_like(sol_ref)
+    sign[own] = 1.0 - 2.0 * bits[...].astype(jnp.float32)
+    begin(2, 0)
+
     me = (at["gx"] * sizes["gy"] + at["gy"]) * sizes["gz"] + at["gz"]
     lane = lax.broadcasted_iota(jnp.int32, (1, LANES), 1)
 
-    def own_rows(ref):
+    def own_rows(number):
         begin_at = me * share
-        row = ref[pl.ds(begin_at // LANES, 1), :]
+        row = freqs[number, pl.ds(begin_at // LANES, 1), :]
         part = lax.rem(begin_at, LANES) // share
         spread = row
         for k in range(LANES // share):
@@ -303,40 +329,60 @@
             spread = jnp.where(part == k, turned, spread)
         return jnp.concatenate([spread] * (wide // LANES), axis=1)
 
-    group = lax.broadcasted_iota(jnp.int32, (nz, wide), 1) // share
-    cos_z = cosines(own_rows(fz_ref), nz, nz)
-    first = cos_z.astype(jnp.bfloat16).astype(jnp.float32)
-    second = (cos_z - first).astype(jnp.bfloat16).astype(jnp.float32)
-    third = cos_z - first - second
-    chosen = jnp.where(group == 0, first, jnp.where(group == 1, second, third))
-    table[...] = jnp.where(group < 3, chosen, 0.0).astype(jnp.bfloat16)
-    cos_x = cosines(own_rows(fx_ref), nx, nx)
-    cos_y = cosines(own_rows(fy_ref), ny, ny)
-    for x in range(nx):
-        weights[x] = cos_x[x : x + 1] * cos_y
-    edge = jnp.zeros((ny, nz), jnp.float32)
-    for j in range(BASIS):
-        vectors[j, 0] = edge
-        vectors[j, nx + 1] = edge
-
-    for copy in arriving:
-        copy.wait_recv()
+    def tables():
+        cos_x = cosines(own_rows(0), nx, nx)
+        cos_y = cosines(own_rows(1), ny, ny)
+        for x in range(nx):
+            weights[x] = cos_x[x : x + 1] * cos_y
+        group = lax.broadcasted_iota(jnp.int32, (nz, wide), 1) // share
+        cos_z = cosines(own_rows(2), nz, nz)
+        first = cos_z.astype(jnp.bfloat16).astype(jnp.float32)
+        second = (cos_z - first).astype(jnp.bfloat16).astype(jnp.float32)
+        third = cos_z - first - second
+        chosen = jnp.where(group == 0, first, jnp.where(group == 1, second, third))
+        table[...] = jnp.where(group < 3, chosen, 0.0).astype(jnp.bfloat16)
+
     for step in range(1, 4):
-        for copy in begin(step):
-            copy.wait_recv()
+        for array in range(2):
+            arrive(array, step - 1)
+            begin(array, step)
+        if step == 1:
+            tables()
+    arrive(0, 3)
+    arrive(1, 3)
 
     row_at = lax.broadcasted_iota(jnp.int32, (ny, nz), 0)
     lane_at = lax.broadcasted_iota(jnp.int32, (ny, nz), 1)
 
-    def put_flipped(x, plane):
-        turned = plane * sign[x]
+    def vector(j):
+        return field if j == 0 else vectors.at[j - 1]
+
+    def stencil_step(j):
+        here_ref = vector(j)
+        for x in range(nx):
+            here = here_ref[x]
+            beside = None
+            for near in (x + 1, x - 1):
+                if 0 <= near < nx:
+                    beside = here_ref[near] if beside is None else beside + here_ref[near]
+            beside = beside + jnp.where(row_at < ny - 1, pltpu.roll(here, ny - 1, 0), 0.0)
+            beside = beside + jnp.where(row_at > 0, pltpu.roll(here, 1, 0), 0.0)
+            beside = beside + jnp.where(lane_at < nz - 1, pltpu.roll(here, nz - 1, 1), 0.0)
+            beside = beside + jnp.where(lane_at > 0, pltpu.roll(here, 1, 1), 0.0)
+            image = (6.0 + diag[x]) * here - beside
+            images[j, x] = image
+            if j + 1 < BASIS:
+                turned = image - center_value * here
+                if j == 0:
+                    vectors[j, x] = turned * (1.0 / half_range)
+                else:
+                    vectors[j, x] = turned * (2.0 / half_range) - vector(j - 1)[x]
+
+    def sketch_row(j):
+        turned = (images[j] * sign[...]).reshape(cells, nz)
         high = turned.astype(jnp.bfloat16)
-        flipped[0, x] = high
-        flipped[1, x] = (turned - high.astype(jnp.float32)).astype(jnp.bfloat16)
-
-    def sketch_row(j):
-        cells = nx * ny
-        both = flipped[...].reshape(2 * cells, nz)
+        low = (turned - high.astype(jnp.float32)).astype(jnp.bfloat16)
+        both = jnp.concatenate([high, low], axis=0)
         sampled = jnp.dot(both, table[...], preferred_element_type=jnp.float32)
         sampled = (sampled[:cells] + sampled[cells:]) * weights[...].reshape(cells, wide)
         total = jnp.sum(sampled, axis=0, keepdims=True)
@@ -348,41 +394,23 @@
             spread = spread + pltpu.roll(folded, k * share, 1)
         rows[pl.ds(j, 1), :] = spread
 
-    small = 0
-    for restart in range(ITERS):
-
-        @pl.loop(0, nx)
-        def _(x):
-            plane = field[x]
-            vectors[0, x + 1] = plane
-            put_flipped(x, plane)
-
-        sketch_row(BASIS)
-
-        @pl.loop(0, BASIS)
+    @pl.loop(0, ITERS)
+    def _(restart):
+        for j in range(BASIS):
+            stencil_step(j)
+            if j in (1, 3, 5):
+
+                @pl.when(restart == 0)
+                def _():
+                    arrive(2, j // 2)
+                    begin(2, j // 2 + 1)
+
+        @pl.when(restart == 0)
+        def _():
+            arrive(2, 3)
+
+        @pl.loop(0, BASIS + 1, unroll=3)
         def _(j):
-            before = jnp.maximum(j - 1, 0)
-            after = jnp.minimum(j + 1, BASIS - 1)
-            step = jnp.where(j == 0, 1.0 / half_range, 2.0 / half_range).astype(jnp.float32)
-            old = jnp.where(j == 0, 0.0, 1.0).astype(jnp.float32)
-
-            @pl.loop(0, nx, unroll=2)
-            def _(x):
-                here = vectors[j, x + 1]
-                beside = vectors[j, x + 2] + vectors[j, x]
-                beside = beside + jnp.where(row_at < ny - 1, pltpu.roll(here, ny - 1, 0), 0.0)
-                beside = beside + jnp.where(row_at > 0, pltpu.roll(here, 1, 0), 0.0)
-                beside = beside + jnp.where(lane_at < nz - 1, pltpu.roll(here, nz - 1, 1), 0.0)
-                beside = beside + jnp.where(lane_at > 0, pltpu.roll(here, 1, 1), 0.0)
-                image = (6.0 + diag[x]) * here - beside
-                images[j, x] = image
-                put_flipped(x, image)
-                turned = (image - center_value * here) * step - old * vectors[before, x + 1]
-
-                @pl.when(j < BASIS - 1)
-                def _():
-                    vectors[after, x + 1] = turned
-
             sketch_row(j)
 
         buffer = sums.at[restart]
@@ -392,6 +420,8 @@
             1, 1, 1, BASIS, LANES
         )
         whole = {axis: False for axis in sizes}
+        small = restart * sum(size - 1 for size in sizes.values())
+        started = []
         for axis in ("gy", "gx", "gz"):
             here, size = at[axis], sizes[axis]
             arrivals = []
@@ -399,7 +429,7 @@
                 target, origin = lax.rem(here + k, size), lax.rem(here + size - k, size)
                 sems = dict(send_sem=small_send.at[small], recv_sem=small_recv.at[small])
                 go = dict(device_id={axis: target}, device_id_type=MESH)
-                small += 1
+                small = small + 1
                 source, landing = (
                     buffer.at[
                         tuple(
@@ -411,7 +441,7 @@
                 )
                 copy = pltpu.make_async_remote_copy(src_ref=source, dst_ref=source, **sems, **go)
                 copy.start()
-                gather.started.append(copy)
+                started.append(copy)
                 arrivals.append(
                     pltpu.make_async_remote_copy(src_ref=landing, dst_ref=landing, **sems, **go)
                 )
@@ -423,31 +453,35 @@
         sketched = [jnp.where(lane < share, tiles[:, j, :], 0.0) for j in range(BASIS)]
         aside = pltpu.roll(tiles[:, 0, :], LANES - share, 1)
         solved = solve_rows(sketched, jnp.where(lane < share, aside, 0.0))
-
-        kept = (pl.ds(x0 + 1, bx), pl.ds(y0, by), pl.ds(z0, bz))
-        total = jnp.zeros((bx, by, bz), jnp.float32) if restart == 0 else sol_ref[...]
+        for copy in started:
+            copy.wait_send()
+
+        total = sol_ref[...]
         for j in range(BASIS):
-            total = total + solved[j].reshape(1, 1, 1) * vectors[(j,) + kept]
+            total = total + solved[j].reshape(1, 1, 1) * vector(j)[own]
         sol_ref[...] = total
-        if restart == ITERS - 1:
+
+        @pl.when(restart == 0)
+        def _():
+            for plan in plans:
+                for sends, _ in plan:
+                    for copy in sends:
+                        copy.wait_send()
+
+        @pl.when(restart == ITERS - 1)
+        def _():
             left = field[own]
             for j in range(BASIS):
                 left = left - solved[j].reshape(1, 1, 1) * images[(j,) + own]
             res_ref[...] = left
-        else:
-            for copy in gather.started:
-                copy.wait_send()
-            gather.started = []
-
-            @pl.loop(0, nx)
-            def _(x):
+
+        @pl.when(restart < ITERS - 1)
+        def _():
+            for x in range(nx):
                 left = field[x]
                 for j in range(BASIS):
                     left = left - solved[j] * images[j, x]
                 field[x] = left
-
-    for copy in gather.started:
-        copy.wait_send()
 
 
 def whole_fits(sizes, nx, ny, nz, sampled):
@@ -472,19 +506,20 @@
     return pl.pallas_call(
         functools.partial(whole_kernel, sizes, share),
         out_shape=[jax.ShapeDtypeStruct(block, f32)] * 2,
-        in_specs=[pl.BlockSpec(memory_space=pltpu.VMEM)] * 6,
+        in_specs=[pl.BlockSpec(memory_space=pl.ANY)] * 6,
         out_specs=[pl.BlockSpec(memory_space=pltpu.VMEM)] * 2,
         scratch_shapes=[
+            pltpu.VMEM((BASIS + 1, nx, ny, nz), f32),
             pltpu.VMEM((nx, ny, nz), f32),
             pltpu.VMEM((nx, ny, nz), f32),
-            pltpu.VMEM((nx, ny, nz), f32),
-            pltpu.VMEM((BASIS, nx + 2, ny, nz), f32),
-            pltpu.VMEM((BASIS, nx, ny, nz), f32),
-            pltpu.VMEM((2, nx, ny, nz), jnp.bfloat16),
+            pltpu.VMEM((BASIS - 1, nx, ny, nz), f32),
             pltpu.VMEM((nz, wide), jnp.bfloat16),
             pltpu.VMEM((nx, ny, wide), f32),
             pltpu.VMEM((16, LANES), f32),
             pltpu.VMEM((ITERS, sizes["gy"], sizes["gx"], sizes["gz"], BASIS, LANES), f32),
+            pltpu.VMEM(block, jnp.int32),
+            pltpu.VMEM((3,) + freqs[0].shape, jnp.int32),
+            pltpu.SemaphoreType.DMA((6,)),
             pltpu.SemaphoreType.DMA((copies,)),
             pltpu.SemaphoreType.DMA((copies,)),
             pltpu.SemaphoreType.DMA((smalls,)),

time: 87 us -> 66.7 us (0.77)
  Pallas kernels: 80.3 us -> 60.1 us
    pallas_call x1, Pallas kernels: 80.3 us -> 60.1 us  [whole_shards(): pl.pallas_call(functools.partial(whole_kernel, sizes, share), out_shape=[...]
where the time goes in v2:
time: 66.7 us; the launch traced here: 66.2 us
  Pallas kernels  60.1 us (90%)
  local copies, waits for them, and re-layouts  5.45 us (8%)
    pallas_call x1, Pallas kernels, whole_shards(): pl.pallas_call(functools.partial(whole_kernel, sizes, share), out_shape=[...  60.1 us
    unnamed x14, local copies, waits for them, and re-layouts  5.45 us

profile of v2, /device:TPU:0, one launch (start us, length us, event | category | flops | bytes accessed | tf_op | source)
XLA Modules:
  0.0 66.2 jit_solution(15715399770933342971)
XLA Ops:
  0.6 0.0 copy-start
  0.6 0.7 %copy-done = f32[4,8,128]{2,1,0:T(8,128)S(1)} copy-done((f32[4,8,128]{2,1,0:T(8,128)S(1)}, f32[4,8,128]{2,1,0:T(8,128)}, u32[]{:S(2)}) %copy-start) | copy-done | bytes 16408
  1.4 0.0 copy-start.1
  1.4 0.7 %copy-done.1 = f32[4,8,128]{2,1,0:T(8,128)S(1)} copy-done((f32[4,8,128]{2,1,0:T(8,128)S(1)}, f32[4,8,128]{2,1,0:T(8,128)}, u32[]{:S(2)}) %copy-start.1) | copy-done | bytes 16408
  2.1 0.0 copy-start.2
  2.1 0.7 %copy-done.2 = s32[4,8,128]{2,1,0:T(8,128)S(1)} copy-done((s32[4,8,128]{2,1,0:T(8,128)S(1)}, s32[4,8,128]{2,1,0:T(8,128)}, u32[]{:S(2)}) %copy-start.2) | copy-done | bytes 16408
  2.8 0.0 copy-start.3
  2.8 0.7 %copy-done.3 = s32[2048]{0:T(1024)S(1)} copy-done((s32[2048]{0:T(1024)S(1)}, s32[2048]{0:T(1024)}, u32[]{:S(2)}) %copy-start.3) | copy-done | bytes 8216
  3.5 0.0 copy-start.4
  3.5 0.7 %copy-done.4 = s32[2048]{0:T(1024)S(1)} copy-done((s32[2048]{0:T(1024)S(1)}, s32[2048]{0:T(1024)}, u32[]{:S(2)}) %copy-start.4) | copy-done | bytes 8216
  4.2 0.0 copy-start.5
  4.2 0.7 %copy-done.5 = s32[2048]{0:T(1024)S(1)} copy-done((s32[2048]{0:T(1024)S(1)}, s32[2048]{0:T(1024)}, u32[]{:S(2)}) %copy-start.5) | copy-done | bytes 8216
  4.9 60.1 %shard_map.77 = (f32[4,8,128]{2,1,0:T(8,128)S(1)}, f32[4,8,128]{2,1,0:T(8,128)S(1)}) custom-call(f32[4,8,128]{2,1,0:T(8,128)S(1)} %copy-done, f32[4,8,128]{2,1,0:T(8,128)S(1)} %copy-done.1, s32[4,8,128]{2,1,0:T(8,128)S(1)} %copy-done.2, s32[16,128]{1,0:T(8,128)S(1)} %bitcast.3, s32[16,128]{1,0:T(8,128)S(1)} %bitcast.4, s32[16,128]{1,0:T(8,128)S(1)} %bitcast.5), custom_call_target="tpu_custom_call" | custom-call | tf_op jit(solution)/shard_map/pallas_call | solution.py:506
  64.9 0.6 copy.10
  65.5 0.6 copy.11
Async XLA Ops:
  0.6 0.7 %copy-start = (f32[4,8,128]{2,1,0:T(8,128)S(1)}, f32[4,8,128]{2,1,0:T(8,128)}, u32[]{:S(2)}) copy-start(f32[4,8,128]{2,1,0:T(8,128)} %right_ref.1) | copy-start | bytes 49156
  1.4 0.7 %copy-start.1 = (f32[4,8,128]{2,1,0:T(8,128)S(1)}, f32[4,8,128]{2,1,0:T(8,128)}, u32[]{:S(2)}) copy-start(f32[4,8,128]{2,1,0:T(8,128)} %diagonal_ref.1) | copy-start | bytes 49156
  2.1 0.7 %copy-start.2 = (s32[4,8,128]{2,1,0:T(8,128)S(1)}, s32[4,8,128]{2,1,0:T(8,128)}, u32[]{:S(2)}) copy-start(s32[4,8,128]{2,1,0:T(8,128)} %bits_ref.1) | copy-start | bytes 49156
  2.8 0.7 %copy-start.3 = (s32[2048]{0:T(1024)S(1)}, s32[2048]{0:T(1024)}, u32[]{:S(2)}) copy-start(s32[2048]{0:T(1024)} %param.9) | copy-start | bytes 24580
  3.5 0.7 %copy-start.4 = (s32[2048]{0:T(1024)S(1)}, s32[2048]{0:T(1024)}, u32[]{:S(2)}) copy-start(s32[2048]{0:T(1024)} %param.10) | copy-start | bytes 24580
  4.2 0.7 %copy-start.5 = (s32[2048]{0:T(1024)S(1)}, s32[2048]{0:T(1024)}, u32[]{:S(2)}) copy-start(s32[2048]{0:T(1024)} %param.11) | copy-start | bytes 24580

commit v3 on v2

--- a/solution.py
+++ b/solution.py
@@ -154,28 +154,47 @@
     return jnp.sum(jnp.sum(value, axis=0, keepdims=True), axis=1, keepdims=True)
 
 
+def swept(left, among, short):
+    count, left, amounts = len(left), list(left), []
+    for e in range(count):
+        amount = left[e]
+        amounts.append(amount)
+        left[e] = amount * short[e]
+        for f in range(count):
+            if f != e:
+                left[f] = left[f] - amount * among[max(e, f)][min(e, f)]
+    return amounts, left
+
+
 def solve_rows(rows, target):
     count = len(rows)
-    basis, among, short, upper, inverse = [], [], [], {}, []
+    inner = [[total_of(rows[i] * rows[j]) for j in range(i, count)] for i in range(count)]
+    basis, onto, among, short, upper, inverse = [], [], [], [], {}, []
     for at_column in range(count):
-        column = rows[at_column]
-        for repeat in range(2):
-            left = [total_of(q * column) for q in basis]
-            amounts = []
+        column, square, left = rows[at_column], inner[at_column][0], []
+        amounts = [0.0] * at_column
+        if at_column:
+            first, _ = swept([onto[e][at_column] for e in range(at_column)], among, short)
             for e in range(at_column):
-                amount = left[e]
-                amounts.append(amount)
-                left[e] = amount * short[e]
-                for f in range(at_column):
-                    if f != e:
-                        left[f] = left[f] - amount * among[max(e, f)][min(e, f)]
+                column = column - first[e] * basis[e]
+            start = [total_of(q * column) for q in basis]
+            square = total_of(column * column)
+            second, left = swept(start, among, short)
             for e in range(at_column):
-                column = column - amounts[e] * basis[e]
-                upper[e, at_column] = upper.get((e, at_column), 0.0) + amounts[e]
-        length = jnp.sqrt(total_of(column * column) + tiny_value)
-        scale = 1.0 / length
+                column = column - second[e] * basis[e]
+                square = square - second[e] * (start[e] + left[e])
+                amounts[e] = first[e] + second[e]
+                upper[e, at_column] = amounts[e]
+        scale = lax.rsqrt(jnp.maximum(square, 0.0) + tiny_value)
         basis.append(column * scale)
-        among.append([value * scale for value in left] if at_column else [])
+        along = {}
+        for j in range(at_column + 1, count):
+            value = inner[at_column][j - at_column]
+            for e in range(at_column):
+                value = value - amounts[e] * onto[e][j]
+            along[j] = value * scale
+        onto.append(along)
+        among.append([value * scale for value in left])
         short.append(tiny_value * scale * scale)
         inverse.append(scale)
     projected = [total_of(q * target) for q in basis]
@@ -280,12 +299,26 @@
     for copy in loads:
         copy.start()
     barrier = pltpu.get_barrier_semaphore()
-    peers = 0
-    for axis, size in sizes.items():
-        for k in range(1, size):
-            target = lax.rem(at[axis] + k, size)
-            pl.semaphore_signal(barrier, inc=1, device_id={axis: target}, device_id_type=MESH)
-            peers += 1
+    side = sizes["gy"] * sizes["gz"]
+    across = at["gy"] * sizes["gz"] + at["gz"]
+
+    def member(index):
+        return {"gy": lax.div(index, sizes["gz"]), "gz": lax.rem(index, sizes["gz"])}
+
+    plane_hops = [
+        (member(lax.rem(across + k, side)), member(lax.rem(across + side - k, side)))
+        for k in range(1, side)
+    ]
+    line_hops = [
+        (
+            {"gx": lax.rem(at["gx"] + k, sizes["gx"])},
+            {"gx": lax.rem(at["gx"] + sizes["gx"] - k, sizes["gx"])},
+        )
+        for k in range(1, sizes["gx"])
+    ]
+    for target, _ in plane_hops + line_hops:
+        pl.semaphore_signal(barrier, inc=1, device_id=target, device_id_type=MESH)
+    peers = len(plane_hops + line_hops)
 
     gather = Gather(sizes, (bx, by, bz), send_sem, recv_sem)
     plans = []
@@ -416,29 +449,23 @@
         buffer = sums.at[restart]
         behind = (lane // share == 1) & (lax.broadcasted_iota(jnp.int32, (BASIS, LANES), 0) == 0)
         tile = jnp.where(behind, rows[BASIS : BASIS + 1, :], rows[0:BASIS, :])
-        buffer[pl.ds(at["gy"], 1), pl.ds(at["gx"], 1), pl.ds(at["gz"], 1)] = tile.reshape(
+        buffer[pl.ds(at["gx"], 1), pl.ds(at["gy"], 1), pl.ds(at["gz"], 1)] = tile.reshape(
             1, 1, 1, BASIS, LANES
         )
-        whole = {axis: False for axis in sizes}
-        small = restart * sum(size - 1 for size in sizes.values())
+
+        def shares(place, whole):
+            rest = [slice(None)] * 2 if whole else [pl.ds(place[axis], 1) for axis in ("gy", "gz")]
+            return buffer.at[(pl.ds(place["gx"], 1), *rest)]
+
+        small = restart * peers
         started = []
-        for axis in ("gy", "gx", "gz"):
-            here, size = at[axis], sizes[axis]
+        for hops, whole in ((plane_hops, False), (line_hops, True)):
             arrivals = []
-            for k in range(1, size):
-                target, origin = lax.rem(here + k, size), lax.rem(here + size - k, size)
+            for target, origin in hops:
                 sems = dict(send_sem=small_send.at[small], recv_sem=small_recv.at[small])
-                go = dict(device_id={axis: target}, device_id_type=MESH)
+                go = dict(device_id=target, device_id_type=MESH)
                 small = small + 1
-                source, landing = (
-                    buffer.at[
-                        tuple(
-                            slice(None) if whole[name] else pl.ds(place[name], 1)
-                            for name in ("gy", "gx", "gz")
-                        )
-                    ]
-                    for place in (at, {**at, axis: origin})
-                )
+                source, landing = shares(at, whole), shares({**at, **origin}, whole)
                 copy = pltpu.make_async_remote_copy(src_ref=source, dst_ref=source, **sems, **go)
                 copy.start()
                 started.append(copy)
@@ -447,7 +474,6 @@
                 )
             for copy in arrivals:
                 copy.wait_recv()
-            whole[axis] = True
         devices = math.prod(sizes.values())
         tiles = buffer[...].reshape(devices, BASIS, LANES)
         sketched = [jnp.where(lane < share, tiles[:, j, :], 0.0) for j in range(BASIS)]
@@ -502,11 +528,11 @@
     freqs = [f.reshape(-1, LANES) for f in (freq_x, freq_y, freq_z)]
     f32 = jnp.float32
     copies = copies_needed(sizes)
-    smalls = ITERS * sum(size - 1 for size in sizes.values())
+    smalls = ITERS * (sizes["gx"] - 1 + sizes["gy"] * sizes["gz"] - 1)
     return pl.pallas_call(
         functools.partial(whole_kernel, sizes, share),
         out_shape=[jax.ShapeDtypeStruct(block, f32)] * 2,
-        in_specs=[pl.BlockSpec(memory_space=pl.ANY)] * 6,
+        in_specs=[pl.BlockSpec(memory_space=pltpu.HBM)] * 6,
         out_specs=[pl.BlockSpec(memory_space=pltpu.VMEM)] * 2,
         scratch_shapes=[
             pltpu.VMEM((BASIS + 1, nx, ny, nz), f32),
@@ -516,7 +542,7 @@
             pltpu.VMEM((nz, wide), jnp.bfloat16),
             pltpu.VMEM((nx, ny, wide), f32),
             pltpu.VMEM((16, LANES), f32),
-            pltpu.VMEM((ITERS, sizes["gy"], sizes["gx"], sizes["gz"], BASIS, LANES), f32),
+            pltpu.VMEM((ITERS, sizes["gx"], sizes["gy"], sizes["gz"], BASIS, LANES), f32),
             pltpu.VMEM(block, jnp.int32),
             pltpu.VMEM((3,) + freqs[0].shape, jnp.int32),
             pltpu.SemaphoreType.DMA((6,)),
@@ -526,7 +552,7 @@
             pltpu.SemaphoreType.DMA((smalls,)),
         ],
         compiler_params=pltpu.CompilerParams(
-            collective_id=0, has_side_effects=True, vmem_limit_bytes=40 * 1024 * 1024
+            collective_id=0, has_side_effects=True, vmem_limit_bytes=56 * 1024 * 1024
         ),
     )(right_side, diagonal, sign_bits, *freqs)
 

time: 66.7 us -> 58.2 us (0.87)
  Pallas kernels: 60.1 us -> 55.4 us
  local copies, waits for them, and re-layouts: 5.45 us -> 1.94 us
    pallas_call x1, Pallas kernels: 60.1 us -> 55.4 us  [whole_shards(): pl.pallas_call(functools.partial(whole_kernel, sizes, share), out_shape=[...]
    unnamed x14 -> x4, local copies, waits for them, and re-layouts: 5.45 us -> 1.94 us
where the time goes in v3:
time: 58.2 us; the launch traced here: 58 us
  Pallas kernels  55.4 us (95%)
  local copies, waits for them, and re-layouts  1.94 us (3%)
  between operations  0.65 us (1%)
    pallas_call x1, Pallas kernels, whole_shards(): pl.pallas_call(functools.partial(whole_kernel, sizes, share), out_shape=[...  55.4 us
    unnamed x4, local copies, waits for them, and re-layouts  1.94 us

profile of v3, /device:TPU:0, one launch (start us, length us, event | category | flops | bytes accessed | tf_op | source)
XLA Modules:
  0.0 58.0 jit_solution(16786161553309863310)
XLA Ops:
  0.6 55.4 %shard_map.77 = (f32[4,8,128]{2,1,0:T(8,128)}, f32[4,8,128]{2,1,0:T(8,128)}) custom-call(f32[4,8,128]{2,1,0:T(8,128)} %right_ref.1, f32[4,8,128]{2,1,0:T(8,128)} %diagonal_ref.1, s32[4,8,128]{2,1,0:T(8,128)} %bits_ref.1, s32[16,128]{1,0:T(8,128)} %bitcast.3, s32[16,128]{1,0:T(8,128)} %bitcast.4, s32[16,128]{1,0:T(8,128)} %bitcast.5), custom_call_target="tpu_custom_call" | custom-call | tf_op jit(solution)/shard_map/pallas_call | solution.py:532
  56.0 0.0 copy-start
  56.0 1.3 %copy.10 = f32[4,8,128]{2,1,0:T(8,128)} copy(f32[4,8,128]{2,1,0:T(8,128)} %get-tuple-element.4) | data formatting | bytes 32768
  57.4 0.0 copy-done
  57.4 0.6 %copy.11 = f32[4,8,128]{2,1,0:T(8,128)} copy(f32[4,8,128]{2,1,0:T(8,128)S(1)} %copy-done) | data formatting | bytes 32768
Async XLA Ops:
  56.0 1.3 %copy-start = (f32[4,8,128]{2,1,0:T(8,128)S(1)}, f32[4,8,128]{2,1,0:T(8,128)}, u32[]{:S(2)}) copy-start(f32[4,8,128]{2,1,0:T(8,128)} %get-tuple-element.5) | copy-start | bytes 49156

commit v4 on v3

--- a/solution.py
+++ b/solution.py
@@ -225,7 +225,7 @@
             ys = [lax.rem(gy, 2) + 2 * k for k in range(self.sizes["gy"] // 2)]
         return [ref.at[xs, pl.ds(pl.multiple_of(y * by, by), by), zs] for y in ys]
 
-    def plan(self, ref, state, phase):
+    def plan(self, ref, state, phase, held=None):
         axis = {"X": "gx", "Z": "gz", "H": "gy", "C": "gy"}[phase]
         size, here = self.sizes[axis], self.at[axis]
         if phase == "C":
@@ -246,7 +246,9 @@
                 sems = dict(send_sem=self.send_sem.at[n], recv_sem=self.recv_sem.at[n])
                 go = dict(device_id={axis: target}, device_id_type=MESH)
                 sends.append(
-                    pltpu.make_async_remote_copy(src_ref=source, dst_ref=source, **sems, **go)
+                    pltpu.make_async_remote_copy(
+                        src_ref=source if held is None else held, dst_ref=source, **sems, **go
+                    )
                 )
                 arriving.append(
                     pltpu.make_async_remote_copy(src_ref=landing, dst_ref=landing, **sems, **go)
@@ -322,9 +324,15 @@
 
     gather = Gather(sizes, (bx, by, bz), send_sem, recv_sem)
     plans = []
-    for ref, order in [(field, "XZHC"), (diag, "XHZC"), (sign, "XZHC")]:
+    for ref, order, held in [
+        (field, "XZHC", right_ref),
+        (diag, "XHZC", diagonal_ref),
+        (sign, "XZHC", None),
+    ]:
         state = {"x": "own", "y": "own", "z": "own"}
-        plans.append([gather.plan(ref, state, phase) for phase in order])
+        plans.append(
+            [gather.plan(ref, state, phase, held if phase == "X" else None) for phase in order]
+        )
 
     def begin(array, step):
         for copy in plans[array][step][0]:
@@ -334,12 +342,10 @@
         for copy in plans[array][step][1]:
             copy.wait_recv()
 
-    for copy in loads[:2]:
-        copy.wait()
     pl.semaphore_wait(barrier, peers)
     begin(0, 0)
     begin(1, 0)
-    for copy in loads[2:]:
+    for copy in loads:
         copy.wait()
     sol_ref[...] = jnp.zeros_like(sol_ref)
     sign[own] = 1.0 - 2.0 * bits[...].astype(jnp.float32)
@@ -373,7 +379,9 @@
         second = (cos_z - first).astype(jnp.bfloat16).astype(jnp.float32)
         third = cos_z - first - second
         chosen = jnp.where(group == 0, first, jnp.where(group == 1, second, third))
-        table[...] = jnp.where(group < 3, chosen, 0.0).astype(jnp.bfloat16)
+        held = jnp.where(group < 3, chosen, 0.0).astype(jnp.bfloat16)
+        table[0:nz] = held
+        table[nz : 2 * nz] = held
 
     for step in range(1, 4):
         for array in range(2):
@@ -384,8 +392,30 @@
     arrive(0, 3)
     arrive(1, 3)
 
-    row_at = lax.broadcasted_iota(jnp.int32, (ny, nz), 0)
-    lane_at = lax.broadcasted_iota(jnp.int32, (ny, nz), 1)
+    def beside_along_y(plane):
+        tiles = plane.reshape(ny // 8, 8, nz)
+        row_at = lax.broadcasted_iota(jnp.int32, tiles.shape, 1)
+        outside = jnp.zeros((1, 8, nz), jnp.float32)
+        down, up = pltpu.roll(tiles, 1, 1), pltpu.roll(tiles, 7, 1)
+        below = jnp.where(row_at == 0, jnp.concatenate([outside, down[:-1]], axis=0), down)
+        above = jnp.where(row_at == 7, jnp.concatenate([up[1:], outside], axis=0), up)
+        return (below + above).reshape(ny, nz)
+
+    def beside_along_z(plane):
+        parts = nz // LANES
+        lane_at = lax.broadcasted_iota(jnp.int32, (ny, LANES), 1)
+        cut = [plane[:, c * LANES : (c + 1) * LANES] for c in range(parts)]
+        later = [pltpu.roll(part, 1, 1) for part in cut]
+        sooner = [pltpu.roll(part, LANES - 1, 1) for part in cut]
+        summed = []
+        for c in range(parts):
+            low = later[c - 1] if c else 0.0
+            high = sooner[c + 1] if c + 1 < parts else 0.0
+            summed.append(
+                jnp.where(lane_at == 0, low, later[c])
+                + jnp.where(lane_at == LANES - 1, high, sooner[c])
+            )
+        return jnp.concatenate(summed, axis=1)
 
     def vector(j):
         return field if j == 0 else vectors.at[j - 1]
@@ -398,10 +428,7 @@
             for near in (x + 1, x - 1):
                 if 0 <= near < nx:
                     beside = here_ref[near] if beside is None else beside + here_ref[near]
-            beside = beside + jnp.where(row_at < ny - 1, pltpu.roll(here, ny - 1, 0), 0.0)
-            beside = beside + jnp.where(row_at > 0, pltpu.roll(here, 1, 0), 0.0)
-            beside = beside + jnp.where(lane_at < nz - 1, pltpu.roll(here, nz - 1, 1), 0.0)
-            beside = beside + jnp.where(lane_at > 0, pltpu.roll(here, 1, 1), 0.0)
+            beside = beside + beside_along_y(here) + beside_along_z(here)
             image = (6.0 + diag[x]) * here - beside
             images[j, x] = image
             if j + 1 < BASIS:
@@ -415,9 +442,9 @@
         turned = (images[j] * sign[...]).reshape(cells, nz)
         high = turned.astype(jnp.bfloat16)
         low = (turned - high.astype(jnp.float32)).astype(jnp.bfloat16)
-        both = jnp.concatenate([high, low], axis=0)
+        both = jnp.concatenate([high, low], axis=1)
         sampled = jnp.dot(both, table[...], preferred_element_type=jnp.float32)
-        sampled = (sampled[:cells] + sampled[cells:]) * weights[...].reshape(cells, wide)
+        sampled = sampled * weights[...].reshape(cells, wide)
         total = jnp.sum(sampled, axis=0, keepdims=True)
         folded = total[:, :LANES]
         for k in range(1, wide // LANES):
@@ -539,7 +566,7 @@
             pltpu.VMEM((nx, ny, nz), f32),
             pltpu.VMEM((nx, ny, nz), f32),
             pltpu.VMEM((BASIS - 1, nx, ny, nz), f32),
-            pltpu.VMEM((nz, wide), jnp.bfloat16),
+            pltpu.VMEM((2 * nz, wide), jnp.bfloat16),
             pltpu.VMEM((nx, ny, wide), f32),
             pltpu.VMEM((16, LANES), f32),
             pltpu.VMEM((ITERS, sizes["gx"], sizes["gy"], sizes["gz"], BASIS, LANES), f32),

time: 58.2 us -> 58.3 us (level)
  no operation moved by 1% of the time
where the time goes in v4:
time: 58.3 us; the launch traced here: 58 us
  Pallas kernels  55.5 us (95%)
  local copies, waits for them, and re-layouts  1.94 us (3%)
  between operations  0.65 us (1%)
    pallas_call x1, Pallas kernels, whole_shards(): pl.pallas_call(functools.partial(whole_kernel, sizes, share), out_shape=[...  55.5 us
    unnamed x4, local copies, waits for them, and re-layouts  1.94 us

profile of v4, /device:TPU:0, one launch (start us, length us, event | category | flops | bytes accessed | tf_op | source)
XLA Modules:
  0.0 58.0 jit_solution(13410709239834910273)
XLA Ops:
  0.6 55.5 %shard_map.77 = (f32[4,8,128]{2,1,0:T(8,128)}, f32[4,8,128]{2,1,0:T(8,128)}) custom-call(f32[4,8,128]{2,1,0:T(8,128)} %right_ref.1, f32[4,8,128]{2,1,0:T(8,128)} %diagonal_ref.1, s32[4,8,128]{2,1,0:T(8,128)} %bits_ref.1, s32[16,128]{1,0:T(8,128)} %bitcast.3, s32[16,128]{1,0:T(8,128)} %bitcast.4, s32[16,128]{1,0:T(8,128)} %bitcast.5), custom_call_target="tpu_custom_call" | custom-call | tf_op jit(solution)/shard_map/pallas_call | solution.py:559
  56.1 0.0 copy-start
  56.1 1.3 %copy.10 = f32[4,8,128]{2,1,0:T(8,128)} copy(f32[4,8,128]{2,1,0:T(8,128)} %get-tuple-element.4) | data formatting | bytes 32768
  57.4 0.0 copy-done
  57.4 0.6 %copy.11 = f32[4,8,128]{2,1,0:T(8,128)} copy(f32[4,8,128]{2,1,0:T(8,128)S(1)} %copy-done) | data formatting | bytes 32768
Async XLA Ops:
  56.1 1.3 %copy-start = (f32[4,8,128]{2,1,0:T(8,128)S(1)}, f32[4,8,128]{2,1,0:T(8,128)}, u32[]{:S(2)}) copy-start(f32[4,8,128]{2,1,0:T(8,128)} %get-tuple-element.5) | copy-start | bytes 49156

commit v5 on v4

--- a/solution.py
+++ b/solution.py
@@ -271,7 +271,7 @@
 
 def whole_kernel(
     sizes, share, right_ref, diagonal_ref, bits_ref, fx_ref, fy_ref, fz_ref, sol_ref, res_ref,
-    images, diag, sign, vectors, table, weights, rows, sums, bits, freqs, load_sem, send_sem,
+    images, diag, sign, even, odd, kept, table, weights, rows, sums, bits, freqs, load_sem, send_sem,
     recv_sem, small_send, small_recv,
 ):
     bx, by, bz = right_ref.shape
@@ -417,11 +417,9 @@
             )
         return jnp.concatenate(summed, axis=1)
 
-    def vector(j):
-        return field if j == 0 else vectors.at[j - 1]
-
-    def stencil_step(j):
-        here_ref = vector(j)
+    def stencil_step(j, here_ref, other_ref):
+        factor = jnp.where(j == 0, 1.0 / half_range, 2.0 / half_range).astype(jnp.float32)
+        kept[j] = here_ref[own]
         for x in range(nx):
             here = here_ref[x]
             beside = None
@@ -431,12 +429,7 @@
             beside = beside + beside_along_y(here) + beside_along_z(here)
             image = (6.0 + diag[x]) * here - beside
             images[j, x] = image
-            if j + 1 < BASIS:
-                turned = image - center_value * here
-                if j == 0:
-                    vectors[j, x] = turned * (1.0 / half_range)
-                else:
-                    vectors[j, x] = turned * (2.0 / half_range) - vector(j - 1)[x]
+            other_ref[x] = (image - center_value * here) * factor - other_ref[x]
 
     def sketch_row(j):
         turned = (images[j] * sign[...]).reshape(cells, nz)
@@ -456,14 +449,20 @@
 
     @pl.loop(0, ITERS)
     def _(restart):
-        for j in range(BASIS):
-            stencil_step(j)
-            if j in (1, 3, 5):
-
-                @pl.when(restart == 0)
+        for x in range(nx):
+            even[x] = field[x]
+            odd[x] = jnp.zeros((ny, nz), jnp.float32)
+
+        @pl.loop(0, BASIS // 2)
+        def _(pair):
+            stencil_step(2 * pair, even, odd)
+            stencil_step(2 * pair + 1, odd, even)
+            for step in range(3):
+
+                @pl.when((restart == 0) & (pair == step))
                 def _():
-                    arrive(2, j // 2)
-                    begin(2, j // 2 + 1)
+                    arrive(2, step)
+                    begin(2, step + 1)
 
         @pl.when(restart == 0)
         def _():
@@ -511,7 +510,7 @@
 
         total = sol_ref[...]
         for j in range(BASIS):
-            total = total + solved[j].reshape(1, 1, 1) * vector(j)[own]
+            total = total + solved[j].reshape(1, 1, 1) * kept[j]
         sol_ref[...] = total
 
         @pl.when(restart == 0)
@@ -565,7 +564,9 @@
             pltpu.VMEM((BASIS + 1, nx, ny, nz), f32),
             pltpu.VMEM((nx, ny, nz), f32),
             pltpu.VMEM((nx, ny, nz), f32),
-            pltpu.VMEM((BASIS - 1, nx, ny, nz), f32),
+            pltpu.VMEM((nx, ny, nz), f32),
+            pltpu.VMEM((nx, ny, nz), f32),
+            pltpu.VMEM((BASIS,) + block, f32),
             pltpu.VMEM((2 * nz, wide), jnp.bfloat16),
             pltpu.VMEM((nx, ny, wide), f32),
             pltpu.VMEM((16, LANES), f32),

time: 58.3 us -> 58.5 us (level)
  no operation moved by 1% of the time
where the time goes in v5:
time: 58.5 us; the launch traced here: 58.3 us
  Pallas kernels  55.7 us (95%)
  local copies, waits for them, and re-layouts  1.94 us (3%)
  between operations  0.65 us (1%)
    pallas_call x1, Pallas kernels, whole_shards(): pl.pallas_call(functools.partial(whole_kernel, sizes, share), out_shape=[...  55.7 us
    unnamed x4, local copies, waits for them, and re-layouts  1.94 us

profile of v5, /device:TPU:0, one launch (start us, length us, event | category | flops | bytes accessed | tf_op | source)
XLA Modules:
  0.0 58.3 jit_solution(17249332272736852503)
XLA Ops:
  0.6 55.7 %shard_map.77 = (f32[4,8,128]{2,1,0:T(8,128)}, f32[4,8,128]{2,1,0:T(8,128)}) custom-call(f32[4,8,128]{2,1,0:T(8,128)} %right_ref.1, f32[4,8,128]{2,1,0:T(8,128)} %diagonal_ref.1, s32[4,8,128]{2,1,0:T(8,128)} %bits_ref.1, s32[16,128]{1,0:T(8,128)} %bitcast.3, s32[16,128]{1,0:T(8,128)} %bitcast.4, s32[16,128]{1,0:T(8,128)} %bitcast.5), custom_call_target="tpu_custom_call" | custom-call | tf_op jit(solution)/shard_map/pallas_call | solution.py:558
  56.4 0.0 copy-start
  56.4 1.3 %copy.10 = f32[4,8,128]{2,1,0:T(8,128)} copy(f32[4,8,128]{2,1,0:T(8,128)} %get-tuple-element.4) | data formatting | bytes 32768
  57.7 0.0 copy-done
  57.7 0.6 %copy.11 = f32[4,8,128]{2,1,0:T(8,128)} copy(f32[4,8,128]{2,1,0:T(8,128)S(1)} %copy-done) | data formatting | bytes 32768
Async XLA Ops:
  56.4 1.3 %copy-start = (f32[4,8,128]{2,1,0:T(8,128)S(1)}, f32[4,8,128]{2,1,0:T(8,128)}, u32[]{:S(2)}) copy-start(f32[4,8,128]{2,1,0:T(8,128)} %get-tuple-element.5) | copy-start | bytes 49156

commit v6 on v5

--- a/solution.py
+++ b/solution.py
@@ -468,7 +468,7 @@
         def _():
             arrive(2, 3)
 
-        @pl.loop(0, BASIS + 1, unroll=3)
+        @pl.loop(0, BASIS + 1, unroll=BASIS + 1)
         def _(j):
             sketch_row(j)
 

time: 58.5 us -> 57.6 us (0.985)
  Pallas kernels: 55.7 us -> 54.7 us
    pallas_call x1, Pallas kernels: 55.7 us -> 54.7 us  [whole_shards(): pl.pallas_call(functools.partial(whole_kernel, sizes, share), out_shape=[...]
where the time goes in v6:
time: 57.6 us; the launch traced here: 57.3 us
  Pallas kernels  54.7 us (95%)
  local copies, waits for them, and re-layouts  1.94 us (3%)
  between operations  0.65 us (1%)
    pallas_call x1, Pallas kernels, whole_shards(): pl.pallas_call(functools.partial(whole_kernel, sizes, share), out_shape=[...  54.7 us
    unnamed x4, local copies, waits for them, and re-layouts  1.94 us

profile of v6, /device:TPU:0, one launch (start us, length us, event | category | flops | bytes accessed | tf_op | source)
XLA Modules:
  0.0 57.3 jit_solution(9397374812254167597)
XLA Ops:
  0.6 54.7 %shard_map.77 = (f32[4,8,128]{2,1,0:T(8,128)}, f32[4,8,128]{2,1,0:T(8,128)}) custom-call(f32[4,8,128]{2,1,0:T(8,128)} %right_ref.1, f32[4,8,128]{2,1,0:T(8,128)} %diagonal_ref.1, s32[4,8,128]{2,1,0:T(8,128)} %bits_ref.1, s32[16,128]{1,0:T(8,128)} %bitcast.3, s32[16,128]{1,0:T(8,128)} %bitcast.4, s32[16,128]{1,0:T(8,128)} %bitcast.5), custom_call_target="tpu_custom_call" | custom-call | tf_op jit(solution)/shard_map/pallas_call | solution.py:558
  55.4 0.0 copy-start
  55.4 1.3 %copy.10 = f32[4,8,128]{2,1,0:T(8,128)} copy(f32[4,8,128]{2,1,0:T(8,128)} %get-tuple-element.4) | data formatting | bytes 32768
  56.7 0.0 copy-done
  56.7 0.6 %copy.11 = f32[4,8,128]{2,1,0:T(8,128)} copy(f32[4,8,128]{2,1,0:T(8,128)S(1)} %copy-done) | data formatting | bytes 32768
Async XLA Ops:
  55.4 1.3 %copy-start = (f32[4,8,128]{2,1,0:T(8,128)S(1)}, f32[4,8,128]{2,1,0:T(8,128)}, u32[]{:S(2)}) copy-start(f32[4,8,128]{2,1,0:T(8,128)} %get-tuple-element.5) | copy-start | bytes 49156
